TPU v7x, 32 devices: a whole 2x2x4 slice. The times are simulated.
32 devices in a mesh: groups: 2 (over x), blk: 4 (over y, core), tok: 4 (over z).
Axes of the slice: x: 2, y: 2, z: 4, core: 2. Of those that a mesh axis runs over, the one named last changes fastest.
Arguments:
- latent_codes: bfloat16 [512, 2, 16, 512], P(('groups', 'tok'), None, 'blk'), parts along dimension 0, may hold values from 0.049804688 to 0.5
- block_lists: int32 [16, 2, 16, 8], P('groups', None, 'blk'), parts along dimension 0, may hold values from 0 to 15, as said below
- block_counts: int32 [16, 2, 16], P('groups', None, 'blk'), parts along dimension 0, may hold values from 1 to 8, as said below
- decoder: bfloat16 [3, 16384, 8192], P(None, 'blk', 'tok'), may hold values from -0.29882812 to 0.29882812
- targets: bfloat16 [512, 2, 8192], P(('groups', 'blk'), None, 'tok'), parts along dimension 0, may hold values from -6 to 6
Outputs:
- recon_error: bfloat16 [512, 2, 8192], P(('groups', 'blk'), None, 'tok'), parts along dimension 0
- decoder_grad: bfloat16 [6, 16384, 8192], P('groups', 'blk', 'tok'), parts along dimension 0
- code_grad: bfloat16 [512, 2, 16, 512], P(('groups', 'tok'), None, 'blk'), parts along dimension 0
There are 2 independent parts, one for each index of `groups`. A program takes and returns all parts, laid end to end along the dimension named above; an argument that names none is the same for every part. Nothing has to cross between parts.
Inputs may be any that keep to these rules, and one draw needn't show every extreme that they name: `block_lists`: within one tile, source layer and region the 8 listed block numbers are distinct; only the first block_counts of them are active, the others are ignored. `block_counts`: 8 is reached in every draw.
All inputs are finite; a program needn't handle non-finite values.
Results may differ from a plain program's by a relative error of at most 0.014.
Values may be sent and summed in bfloat16 or wider, within the bound.
A program may use at most 320 MiB of HBM per device.

v0:
```python
import functools

import jax
import jax.numpy as jnp
from jax import lax
from jax.experimental import pallas as pl
from jax.experimental.pallas import tpu as pltpu
from jax.sharding import PartitionSpec as P

BLOCK = 64
PAIR = 2 * BLOCK
VMEM_LIMIT = 40 * 2**20


def params(dims):
    return pltpu.CompilerParams(
        dimension_semantics=("arbitrary",) * dims, vmem_limit_bytes=VMEM_LIMIT
    )


def cost(flops, read):
    return pl.CostEstimate(flops=flops, bytes_accessed=read, transcendentals=0)


def pick_blocks(read_pair, write_pair, index, dup, sources, dests, rows):
    low = lax.broadcasted_iota(jnp.int32, (rows, PAIR), 1) < BLOCK
    for j in range(sources // 2):
        value = read_pair(j)
        turned = pltpu.roll(value, BLOCK, 1)
        dup[2 * j] = jnp.where(low, value, turned)
        dup[2 * j + 1] = jnp.where(low, turned, value)
    dup[sources] = jnp.zeros((rows, PAIR), jnp.float32)
    for j in range(dests // 2):
        write_pair(j, jnp.where(low, dup[index(2 * j)], dup[index(2 * j + 1)]))


def expand_kernel(rows, slots, blocks, inverse, order, src, out, dup):
    step = pl.program_id(0)
    regions = src.shape[1]
    tiles = src.shape[2] // rows
    first = order[step] * tiles
    width = blocks * BLOCK
    for r in range(regions):
        for x in range(tiles):
            here = pl.ds(x * rows, rows)
            base = ((first + x) * regions + r) * blocks

            def read(j):
                return src[0, r, here, pl.ds(j * PAIR, PAIR)].astype(jnp.float32)

            def write(j, value):
                out[here, pl.ds(r * width + j * PAIR, PAIR)] = value.astype(out.dtype)

            pick_blocks(read, write, lambda k: inverse[base + k], dup.at[r * tiles + x], slots, blocks, rows)


def expand(shards, inverse, order, rows, blocks):
    count, regions, own, slot_width = shards.shape
    slots = slot_width // BLOCK
    width = regions * blocks * BLOCK
    return pl.pallas_call(
        functools.partial(expand_kernel, rows, slots, blocks),
        grid_spec=pltpu.PrefetchScalarGridSpec(
            num_scalar_prefetch=2,
            grid=(count,),
            in_specs=[pl.BlockSpec((1, regions, own, slot_width), lambda k, inv, order: (k, 0, 0, 0))],
            out_specs=pl.BlockSpec((own, width), lambda k, inv, order: (order[k], 0)),
            scratch_shapes=[pltpu.VMEM((regions * own // rows, slots + 1, rows, PAIR), jnp.float32)],
        ),
        out_shape=jax.ShapeDtypeStruct((count * own, width), jnp.bfloat16),
        compiler_params=params(1),
        cost_estimate=cost(0, 6 * count * own * width),
        name="expand",
    )(inverse, order, shards)


def rebuild_kernel(codes, dec, *rest):
    out = rest[-1]
    total = jnp.dot(codes[...], dec[0], preferred_element_type=jnp.float32)
    if len(rest) == 2:
        total = total + rest[0][...]
    out[...] = total.astype(out.dtype)


def rebuild(codes, decoder, pair, before, dtype):
    tokens, latents = codes.shape
    columns = decoder.shape[2]
    wide = min(512, columns)
    tile = pl.BlockSpec((tokens, wide), lambda j: (0, j))
    ins = [codes, decoder] + ([] if before is None else [before])
    return pl.pallas_call(
        rebuild_kernel,
        grid=(columns // wide,),
        in_specs=[
            pl.BlockSpec((tokens, latents), lambda j: (0, 0)),
            pl.BlockSpec((1, latents, wide), lambda j: (pair, 0, j)),
        ] + [tile] * (len(ins) - 2),
        out_specs=tile,
        out_shape=jax.ShapeDtypeStruct((tokens, columns), dtype),
        compiler_params=params(1),
        cost_estimate=cost(2 * tokens * latents * columns, 2 * latents * columns),
        name="rebuild",
    )(*ins)


def outer_kernel(codes, error, *rest):
    out = rest[-1]
    out[0] = lax.dot_general(
        codes[...], error[...], (((0,), (0,)), ((), ())), preferred_element_type=jnp.float32
    ).astype(out.dtype)


def outer(codes, error, pair, pairs, held):
    tokens, latents = codes.shape
    columns = error.shape[1]
    high = min(512, latents)
    ins = [codes, error] + ([] if held is None else [held])
    return pl.pallas_call(
        outer_kernel,
        grid=(latents // high,),
        in_specs=[
            pl.BlockSpec((tokens, high), lambda i: (0, i)),
            pl.BlockSpec((tokens, columns), lambda i: (0, 0)),
        ] + [pl.BlockSpec(memory_space=pl.ANY)] * (len(ins) - 2),
        out_specs=pl.BlockSpec((1, high, columns), lambda i: (pair, i, 0)),
        out_shape=jax.ShapeDtypeStruct((pairs, latents, columns), jnp.bfloat16),
        input_output_aliases={} if held is None else {2: 0},
        compiler_params=params(1),
        cost_estimate=cost(2 * tokens * latents * columns, 2 * latents * columns),
        name="outer",
    )(*ins)


def back_kernel(error, dec, out):
    out[...] = lax.dot_general(
        error[...], dec[0], (((1,), (1,)), ((), ())), preferred_element_type=jnp.float32
    )


def back(error, decoder, pair, region_width):
    tokens, columns = error.shape
    latents = decoder.shape[1]
    return pl.pallas_call(
        back_kernel,
        grid=(latents // region_width,),
        in_specs=[
            pl.BlockSpec((tokens, columns), lambda r: (0, 0)),
            pl.BlockSpec((1, region_width, columns), lambda r: (pair, r, 0)),
        ],
        out_specs=pl.BlockSpec((tokens, region_width), lambda r: (0, r)),
        out_shape=jax.ShapeDtypeStruct((tokens, latents), jnp.float32),
        compiler_params=params(1),
        cost_estimate=cost(2 * tokens * latents * columns, 2 * latents * columns),
        name="back",
    )(error, decoder)


def back_compact_kernel(rows, slots, blocks, regions, chosen, error, dec, *rest):
    out, total, dup = rest[-3:]
    r = pl.program_id(0)
    total[...] = lax.dot_general(
        error[...], dec[0], (((1,), (1,)), ((), ())), preferred_element_type=jnp.float32
    )
    for x in range(total.shape[0] // rows):
        here = pl.ds(x * rows, rows)
        base = (x * regions + r) * slots

        def read(j):
            value = total[here, pl.ds(j * PAIR, PAIR)]
            if len(rest) == 4:
                value = value + rest[0][here, pl.ds(j * PAIR, PAIR)]
            return value

        def write(j, value):
            out[0, here, pl.ds(j * PAIR, PAIR)] = value.astype(out.dtype)

        pick_blocks(read, write, lambda k: chosen[base + k], dup.at[x % 4], blocks, slots, rows)


def back_compact(error, decoder, pair, before, chosen, rows, slots, regions):
    tokens, columns = error.shape
    latents = decoder.shape[1]
    width = latents // regions
    blocks = width // BLOCK
    ins = [error, decoder] + ([] if before is None else [before])
    return pl.pallas_call(
        functools.partial(back_compact_kernel, rows, slots, blocks, regions),
        grid_spec=pltpu.PrefetchScalarGridSpec(
            num_scalar_prefetch=1,
            grid=(regions,),
            in_specs=[
                pl.BlockSpec((tokens, columns), lambda r, ch: (0, 0)),
                pl.BlockSpec((1, width, columns), lambda r, ch: (pair, r, 0)),
            ] + [pl.BlockSpec((tokens, width), lambda r, ch: (0, r))] * (len(ins) - 2),
            out_specs=pl.BlockSpec((1, tokens, slots * BLOCK), lambda r, ch: (r, 0, 0)),
            scratch_shapes=[
                pltpu.VMEM((tokens, width), jnp.float32),
                pltpu.VMEM((4, blocks + 1, rows, PAIR), jnp.float32),
            ],
        ),
        out_shape=jax.ShapeDtypeStruct((regions, tokens, slots * BLOCK), jnp.bfloat16),
        compiler_params=params(1),
        cost_estimate=cost(2 * tokens * latents * columns, 2 * latents * columns),
        name="back_compact",
    )(chosen, *ins)


def gather_tok(own):
    count = lax.axis_size("tok")
    me = lax.axis_index("tok")
    up, down = [own], [own]
    for m in range(1, count):
        up.append(lax.ppermute(up[-1], "tok", [(i, i + 1) for i in range(m - 1, count - 1)]))
        down.append(lax.ppermute(down[-1], "tok", [(i, i - 1) for i in range(1, count - m + 1)]))
    return jnp.stack([own] + [jnp.where(me >= k, up[k], down[count - k]) for k in range(1, count)])


def reduce_tok(parts):
    count = lax.axis_size("tok")
    me = lax.axis_index("tok")

    def chunk(d):
        return lax.dynamic_index_in_dim(parts, d, 1, keepdims=False).astype(jnp.float32)

    own = chunk(me)
    flows = []
    for sign in (1, -1):
        got = None
        for m in range(1, count):
            if sign > 0:
                owner = jnp.minimum(count - m + me, count - 1)
                perm = [(i, i + 1) for i in range(min(m, count - 1))]
            else:
                owner = jnp.maximum(me - (count - m), 0)
                perm = [(count - 1 - i, count - 2 - i) for i in range(min(m, count - 1))]
            send = chunk(owner)
            if got is not None:
                send = send + got.astype(jnp.float32)
            got = lax.ppermute(send.astype(jnp.bfloat16), "tok", perm)
        flows.append(got.astype(jnp.float32))
    return (own + flows[0] + flows[1]).astype(jnp.bfloat16)


def core_swap(value):
    count = lax.axis_size("blk")
    return lax.ppermute(value, "blk", [(i, i ^ 1) for i in range(count)])


def row_shift(value, k):
    count = lax.axis_size("blk")
    return lax.ppermute(value, "blk", [(i, (i + 2 * k) % count) for i in range(count)])


def reduce_blk(part):
    count = lax.axis_size("blk")
    me = lax.axis_index("blk")
    core, row, chips = me % 2, me // 2, count // 2
    tokens, columns = part.shape
    split = part.reshape(chips, 2, tokens // count, columns)
    send = lax.dynamic_index_in_dim(split, 1 - core, 1, keepdims=False)
    kept = lax.dynamic_index_in_dim(split, core, 1, keepdims=False)
    both = kept.astype(jnp.float32) + core_swap(send).astype(jnp.float32)

    def shard(r):
        return lax.dynamic_index_in_dim(both, r, 0, keepdims=False)

    total = shard(row)
    for k in range(1, chips):
        sent = shard((row + k) % chips).astype(jnp.bfloat16)
        total = total + row_shift(sent, k).astype(jnp.float32)
    return total


def gather_blk(own):
    count = lax.axis_size("blk")
    me = lax.axis_index("blk")
    core, row, chips = me % 2, me // 2, count // 2
    held = [own] + [row_shift(own, k) for k in range(1, chips)]
    mine = []
    for r in range(chips):
        value = held[0]
        for k in range(1, chips):
            value = jnp.where((row - k + chips) % chips == r, held[k], value)
        mine.append(value)
    mine = jnp.stack(mine)
    other = core_swap(mine)
    even = jnp.where(core == 0, mine, other)
    odd = jnp.where(core == 0, other, mine)
    return jnp.stack([even, odd], 1).reshape(count * own.shape[0], own.shape[1])


def per_device(latent_codes, block_lists, block_counts, decoder, targets):
    own_rows, layers, regions, slot_width = latent_codes.shape
    slots = block_lists.shape[3]
    latents = decoder.shape[1]
    region_width = latents // regions
    blocks = region_width // BLOCK
    count = lax.axis_size("tok")
    tokens = count * own_rows
    rows = tokens // block_lists.shape[0]
    me = lax.axis_index("tok")

    own = latent_codes.transpose(1, 2, 0, 3)
    gathered = [gather_tok(own[s]) for s in range(layers)]

    active = lax.broadcasted_iota(jnp.int32, block_lists.shape, 3) < block_counts[..., None]
    chosen = jnp.where(active, block_lists, blocks)
    slot = lax.broadcasted_iota(jnp.int32, block_lists.shape + (blocks,), 3)
    block = lax.broadcasted_iota(jnp.int32, block_lists.shape + (blocks,), 4)
    inverse = jnp.min(jnp.where(chosen[..., None] == block, slot, slots), axis=3)
    order = (me - jnp.arange(count, dtype=jnp.int32) + count) % count

    codes = [
        expand(gathered[s], inverse[:, s].reshape(-1), order, rows, blocks) for s in range(layers)
    ]

    part0 = rebuild(codes[0], decoder, 0, None, jnp.bfloat16)
    partial = rebuild(codes[0], decoder, 1, None, jnp.float32)
    part1 = rebuild(codes[1], decoder, 2, partial, jnp.bfloat16)

    def error_of(part, t):
        return (reduce_blk(part) - targets[:, t].astype(jnp.float32)).astype(jnp.bfloat16)

    own_error = [error_of(part0, 0), error_of(part1, 1)]
    recon_error = jnp.stack(own_error, 1)
    error = [gather_blk(e) for e in own_error]

    grads = outer(codes[0], error[0], 0, decoder.shape[0], None)
    early = back(error[0], decoder, 0, region_width)

    def codes_grad(t, pair, before, s):
        packed = back_compact(
            error[t], decoder, pair, before, chosen[:, s].reshape(-1), rows, slots, regions
        )
        return reduce_tok(packed.reshape(regions, count, own_rows, slot_width))

    grad1 = codes_grad(1, 2, None, 1)
    grad0 = codes_grad(1, 1, early, 0)
    grads = outer(codes[0], error[1], 1, decoder.shape[0], grads)
    grads = outer(codes[1], error[1], 2, decoder.shape[0], grads)
    code_grad = jnp.stack([grad0, grad1], 0).transpose(2, 0, 1, 3)
    return (recon_error, grads, code_grad)


def solution(mesh):
    placed = (
        P(("groups", "tok"), None, "blk", None),
        P("groups", None, "blk", None),
        P("groups", None, "blk"),
        P(None, "blk", "tok"),
        P(("groups", "blk"), None, "tok"),
    )
    return jax.shard_map(
        per_device,
        mesh=mesh,
        in_specs=placed,
        out_specs=(
            P(("groups", "blk"), None, "tok"),
            P("groups", "blk", "tok"),
            P(("groups", "tok"), None, "blk", None),
        ),
        check_vma=False,
    )
```

profile of v0, /device:TPU:0, one launch (start us, length us, event | category | flops | bytes accessed | tf_op | source)
XLA Modules:
  0.0 187.2 jit_solution(13916494209195144521)
XLA Ops:
  3.2 5.6 %collective-permute-start = (bf16[4,64,512]{2,1,0:T(8,128)(2,1)S(1)}, bf16[4,64,512]{2,1,0:T(8,128)(2,1)S(1)}, u32[]{:S(2)}, u32[]{:S(2)}) collective-permute-start(bf16[4,64,512]{2,1,0:T(8,128)(2,1)S(1)} %get-tuple-element.34), channel_id=1, source_target_pairs={{0,1},{1,2},{2,3},{4,5},{5,6},{6,7},{8,9},{9,10},{10,11},{12,13},{... | collective-permute-start | bytes 786440 | tf_op jit(solution)/shard_map/ppermute | solution.py:213
  10.1 4.6 %collective-permute-start.8 = (bf16[4,64,512]{2,1,0:T(8,128)(2,1)S(1)}, bf16[4,64,512]{2,1,0:T(8,128)(2,1)S(1)}, u32[]{:S(2)}, u32[]{:S(2)}) collective-permute-start(bf16[4,64,512]{2,1,0:T(8,128)(2,1)S(1)} %get-tuple-element.35), channel_id=1, source_target_pairs={{0,1},{1,2},{2,3},{4,5},{5,6},{6,7},{8,9},{9,10},{10,11},{12,13},{... | collective-permute-start | bytes 786440 | tf_op jit(solution)/shard_map/ppermute | solution.py:213
  15.5 2.1 %fusion.20 = (bf16[64,1,2048]{2,1,0:T(2,128)(2,1)S(1)}, bf16[64,1,2048]{2,1,0:T(2,128)(2,1)S(1)}) fusion(bf16[64,2,2048]{2,1,0:T(2,128)(2,1)} %param.9), kind=kLoop, calls=%fused_computation.101 | loop fusion | bytes 1048576 | tf_op jit(solution)/shard_map/slice | solution.py:322
  23.8 4.0 %collective-permute-done.2 = bf16[4,64,512]{2,1,0:T(8,128)(2,1)S(1)} collective-permute-done((bf16[4,64,512]{2,1,0:T(8,128)(2,1)S(1)}, bf16[4,64,512]{2,1,0:T(8,128)(2,1)S(1)}, u32[]{:S(2)}, u32[]{:S(2)}) %collective-permute-start.2) | collective-permute-done | bytes 262176 | tf_op jit(solution)/shard_map/ppermute | solution.py:214
  29.8 4.3 %collective-permute-done.10 = bf16[4,64,512]{2,1,0:T(8,128)(2,1)S(1)} collective-permute-done((bf16[4,64,512]{2,1,0:T(8,128)(2,1)S(1)}, bf16[4,64,512]{2,1,0:T(8,128)(2,1)S(1)}, u32[]{:S(2)}, u32[]{:S(2)}) %collective-permute-start.10) | collective-permute-done | bytes 262176 | tf_op jit(solution)/shard_map/ppermute | solution.py:214
  36.4 5.8 %collective-permute-done.3 = bf16[4,64,512]{2,1,0:T(8,128)(2,1)S(1)} collective-permute-done((bf16[4,64,512]{2,1,0:T(8,128)(2,1)S(1)}, bf16[4,64,512]{2,1,0:T(8,128)(2,1)S(1)}, u32[]{:S(2)}, u32[]{:S(2)}) %collective-permute-start.3) | collective-permute-done | bytes 262176 | tf_op jit(solution)/shard_map/ppermute | solution.py:214
  42.4 1.8 expand.2.codes
  44.2 8.5 %rebuild.3 = bf16[256,2048]{1,0:T(8,128)(2,1)S(1)} custom-call(bf16[256,4096]{1,0:T(8,128)(2,1)S(1)} %expand.2.codes, bf16[3,4096,2048]{2,1,0:T(8,128)(2,1)} %dec.11), custom_call_target="tpu_custom_call" | custom-call | flops 4294967296 | bytes 16777216 | tf_op jit(solution)/shard_map/rebuild/pallas_call | solution.py:91
  52.7 8.6 %rebuild.4.rest_0_ = f32[256,2048]{1,0:T(8,128)S(1)} custom-call(bf16[256,4096]{1,0:T(8,128)(2,1)S(1)} %expand.2.codes, bf16[3,4096,2048]{2,1,0:T(8,128)(2,1)} %dec.11), custom_call_target="tpu_custom_call" | custom-call | flops 4294967296 | bytes 16777216 | tf_op jit(solution)/shard_map/rebuild/pallas_call | solution.py:91
  63.4 8.6 %rebuild.5 = bf16[256,2048]{1,0:T(8,128)(2,1)S(1)} custom-call(bf16[256,4096]{1,0:T(8,128)(2,1)S(1)} %expand.3.codes, bf16[3,4096,2048]{2,1,0:T(8,128)(2,1)} %dec.11, f32[256,2048]{1,0:T(8,128)S(1)} %rebuild.4.rest_0_), custom_call_target="tpu_custom_call" | custom-call | flops 4294967296 | bytes 16777216 | tf_op jit(solution)/shard_map/rebuild/pallas_call | solution.py:91
  75.9 6.1 %collective-permute-done.7 = bf16[64,2048]{1,0:T(8,128)(2,1)S(1)} collective-permute-done((bf16[64,2048]{1,0:T(8,128)(2,1)S(1)}, bf16[64,2048]{1,0:T(8,128)(2,1)S(1)}, u32[]{:S(2)}, u32[]{:S(2)}) %collective-permute-start.7) | collective-permute-done | bytes 262176 | tf_op jit(solution)/shard_map/ppermute | solution.py:251
  83.9 3.7 %collective-permute-done.15 = bf16[64,2048]{1,0:T(8,128)(2,1)S(1)} collective-permute-done((bf16[64,2048]{1,0:T(8,128)(2,1)S(1)}, bf16[64,2048]{1,0:T(8,128)(2,1)S(1)}, u32[]{:S(2)}, u32[]{:S(2)}) %collective-permute-start.15) | collective-permute-done | bytes 262176 | tf_op jit(solution)/shard_map/ppermute | solution.py:251
  90.9 2.4 %collective-permute-done.18 = bf16[64,2048]{1,0:T(8,128)(2,1)S(1)} collective-permute-done((bf16[64,2048]{1,0:T(8,128)(2,1)S(1)}, bf16[64,2048]{1,0:T(8,128)(2,1)S(1)}, u32[]{:S(2)}, u32[]{:S(2)}) %collective-permute-start.18) | collective-permute-done | bytes 262176 | tf_op jit(solution)/shard_map/ppermute | solution.py:251
  93.4 4.5 %collective-permute-done.16 = bf16[64,2048]{1,0:T(8,128)(2,1)S(1)} collective-permute-done((bf16[64,2048]{1,0:T(8,128)(2,1)S(1)}, bf16[64,2048]{1,0:T(8,128)(2,1)S(1)}, u32[]{:S(2)}, u32[]{:S(2)}) %collective-permute-start.16) | collective-permute-done | bytes 262176 | tf_op jit(solution)/shard_map/ppermute | solution.py:251
  98.4 8.8 %back.1.rest_0_ = f32[256,4096]{1,0:T(8,128)S(1)} custom-call(bf16[256,2048]{1,0:T(8,128)(2,1)S(1)} %bitcast.151, bf16[3,4096,2048]{2,1,0:T(8,128)(2,1)} %dec.11), custom_call_target="tpu_custom_call" | custom-call | flops 4294967296 | bytes 16777216 | tf_op jit(solution)/shard_map/back/pallas_call | solution.py:143
  107.2 9.2 %outer.3.rest_0_ = bf16[3,4096,2048]{2,1,0:T(8,128)(2,1)} custom-call(bf16[256,4096]{1,0:T(8,128)(2,1)S(1)} %expand.2.codes, bf16[256,2048]{1,0:T(8,128)(2,1)S(1)} %bitcast.152), custom_call_target="tpu_custom_call" | custom-call | flops 4294967296 | bytes 16777216 | tf_op jit(solution)/shard_map/outer/pallas_call | solution.py:118
  116.7 9.9 %back_compact.3 = bf16[4,256,512]{2,1,0:T(8,128)(2,1)S(1)} custom-call(s32[256]{0:T(256)S(1)} %reshape_squeeze.15.chosen, bf16[256,2048]{1,0:T(8,128)(2,1)S(1)} %bitcast.147, bf16[3,4096,2048]{2,1,0:T(8,128)(2,1)} %dec.11), custom_call_target="tpu_custom_call" | custom-call | flops 4294967296 | bytes 16777216 | tf_op jit(solution)/shard_map/back_compact/pallas_call | solution.py:186
  129.6 9.9 %back_compact.2 = bf16[4,256,512]{2,1,0:T(8,128)(2,1)S(1)} custom-call(s32[256]{0:T(256)S(1)} %reshape_squeeze.14.chosen, bf16[256,2048]{1,0:T(8,128)(2,1)S(1)} %bitcast.148, bf16[3,4096,2048]{2,1,0:T(8,128)(2,1)} %dec.11, f32[256,4096]{1,0:T(8,128)S(1)} %back.1.rest_0_), custom_call_target="tpu_custom_call" | custom-call | flops 4294967296 | bytes 16777216 | tf_op jit(solution)/shard_map/back_compact/pallas_call | solution.py:186
  142.1 9.2 %outer.4.rest_0_ = bf16[3,4096,2048]{2,1,0:T(8,128)(2,1)} custom-call(bf16[256,4096]{1,0:T(8,128)(2,1)S(1)} %expand.2.codes, bf16[256,2048]{1,0:T(8,128)(2,1)S(1)} %bitcast.149, bf16[3,4096,2048]{2,1,0:T(8,128)(2,1)} %outer.3.rest_0_), custom_call_target="tpu_custom_call", output_to_operand_aliasing={{}: (2, {})} | custom-call | flops 4294967296 | bytes 16777216 | tf_op jit(solution)/shard_map/outer/pallas_call | solution.py:118
  152.5 1.9 %collective-permute-start.27 = (bf16[4,64,512]{2,0,1:T(4,128)(2,1)S(1)}, bf16[4,64,512]{2,0,1:T(4,128)(2,1)S(1)}, u32[]{:S(2)}, u32[]{:S(2)}) collective-permute-start(bf16[4,64,512]{2,0,1:T(4,128)(2,1)S(1)} %fusion.2), channel_id=1, source_target_pairs={{0,1},{1,2},{4,5},{5,6},{8,9},{9,10},{12,13},{13,14},{16,17},{17,1... | collective-permute-start | bytes 786440 | tf_op jit(solution)/shard_map/ppermute | solution.py:239
  155.7 7.0 %collective-permute-start.21 = (bf16[4,64,512]{2,0,1:T(4,128)(2,1)S(1)}, bf16[4,64,512]{2,0,1:T(4,128)(2,1)S(1)}, u32[]{:S(2)}, u32[]{:S(2)}) collective-permute-start(bf16[4,64,512]{2,0,1:T(4,128)(2,1)S(1)} %fusion.8), channel_id=1, source_target_pairs={{0,1},{1,2},{4,5},{5,6},{8,9},{9,10},{12,13},{13,14},{16,17},{17,1... | collective-permute-start | bytes 786440 | tf_op jit(solution)/shard_map/ppermute | solution.py:239
  164.5 5.2 %collective-permute-start.28 = (bf16[4,64,512]{2,0,1:T(4,128)(2,1)S(1)}, bf16[4,64,512]{2,0,1:T(4,128)(2,1)S(1)}, u32[]{:S(2)}, u32[]{:S(2)}) collective-permute-start(bf16[4,64,512]{2,0,1:T(4,128)(2,1)S(1)} %fusion.3), channel_id=1, source_target_pairs={{0,1},{1,2},{2,3},{4,5},{5,6},{6,7},{8,9},{9,10},{10,11},{12,13},{... | collective-permute-start | bytes 786440 | tf_op jit(solution)/shard_map/ppermute | solution.py:239
  171.6 4.6 %collective-permute-start.22 = (bf16[4,64,512]{2,0,1:T(4,128)(2,1)S(1)}, bf16[4,64,512]{2,0,1:T(4,128)(2,1)S(1)}, u32[]{:S(2)}, u32[]{:S(2)}) collective-permute-start(bf16[4,64,512]{2,0,1:T(4,128)(2,1)S(1)} %fusion.9), channel_id=1, source_target_pairs={{0,1},{1,2},{2,3},{4,5},{5,6},{6,7},{8,9},{9,10},{10,11},{12,13},{... | collective-permute-start | bytes 786440 | tf_op jit(solution)/shard_map/ppermute | solution.py:239
  176.2 9.2 %outer.5 = bf16[3,4096,2048]{2,1,0:T(8,128)(2,1)} custom-call(bf16[256,4096]{1,0:T(8,128)(2,1)S(1)} %expand.3.codes, bf16[256,2048]{1,0:T(8,128)(2,1)S(1)} %bitcast.150, bf16[3,4096,2048]{2,1,0:T(8,128)(2,1)} %outer.4.rest_0_), custom_call_target="tpu_custom_call", output_to_operand_aliasing={{}: (2, {})} | custom-call | flops 4294967296 | bytes 16777216 | tf_op jit(solution)/shard_map/outer/pallas_call | solution.py:118
  (109 shorter events, 40.5 us)
Async XLA Ops:
  1.9 16.7 %collective-permute-start.1 = (bf16[4,64,512]{2,1,0:T(8,128)(2,1)S(1)}, bf16[4,64,512]{2,1,0:T(8,128)(2,1)S(1)}, u32[]{:S(2)}, u32[]{:S(2)}) collective-permute-start(bf16[4,64,512]{2,1,0:T(8,128)(2,1)S(1)} %get-tuple-element.34), channel_id=1, source_target_pairs={{1,0},{2,1},{3,2},{5,4},{6,5},{7,6},{9,8},{10,9},{11,10},{13,12},{... | collective-permute-start | bytes 786440 | tf_op jit(solution)/shard_map/ppermute | solution.py:214
  3.2 16.8 %collective-permute-start = (bf16[4,64,512]{2,1,0:T(8,128)(2,1)S(1)}, bf16[4,64,512]{2,1,0:T(8,128)(2,1)S(1)}, u32[]{:S(2)}, u32[]{:S(2)}) collective-permute-start(bf16[4,64,512]{2,1,0:T(8,128)(2,1)S(1)} %get-tuple-element.34), channel_id=1, source_target_pairs={{0,1},{1,2},{2,3},{4,5},{5,6},{6,7},{8,9},{9,10},{10,11},{12,13},{... | collective-permute-start | bytes 786440 | tf_op jit(solution)/shard_map/ppermute | solution.py:213
  8.8 12.6 %collective-permute-start.9 = (bf16[4,64,512]{2,1,0:T(8,128)(2,1)S(1)}, bf16[4,64,512]{2,1,0:T(8,128)(2,1)S(1)}, u32[]{:S(2)}, u32[]{:S(2)}) collective-permute-start(bf16[4,64,512]{2,1,0:T(8,128)(2,1)S(1)} %get-tuple-element.35), channel_id=1, source_target_pairs={{1,0},{2,1},{3,2},{5,4},{6,5},{7,6},{9,8},{10,9},{11,10},{13,12},{... | collective-permute-start | bytes 786440 | tf_op jit(solution)/shard_map/ppermute | solution.py:214
  10.1 12.6 %collective-permute-start.8 = (bf16[4,64,512]{2,1,0:T(8,128)(2,1)S(1)}, bf16[4,64,512]{2,1,0:T(8,128)(2,1)S(1)}, u32[]{:S(2)}, u32[]{:S(2)}) collective-permute-start(bf16[4,64,512]{2,1,0:T(8,128)(2,1)S(1)} %get-tuple-element.35), channel_id=1, source_target_pairs={{0,1},{1,2},{2,3},{4,5},{5,6},{6,7},{8,9},{9,10},{10,11},{12,13},{... | collective-permute-start | bytes 786440 | tf_op jit(solution)/shard_map/ppermute | solution.py:213
  21.4 12.8 %collective-permute-start.10 = (bf16[4,64,512]{2,1,0:T(8,128)(2,1)S(1)}, bf16[4,64,512]{2,1,0:T(8,128)(2,1)S(1)}, u32[]{:S(2)}, u32[]{:S(2)}) collective-permute-start(bf16[4,64,512]{2,1,0:T(8,128)(2,1)S(1)} %collective-permute-done.9), channel_id=1, source_target_pairs={{1,0},{2,1},{5,4},{6,5},{9,8},{10,9},{13,12},{14,13},{17,16},{18,1... | collective-permute-start | bytes 786440 | tf_op jit(solution)/shard_map/ppermute | solution.py:214
  22.7 12.8 %collective-permute-start.12 = (bf16[4,64,512]{2,1,0:T(8,128)(2,1)S(1)}, bf16[4,64,512]{2,1,0:T(8,128)(2,1)S(1)}, u32[]{:S(2)}, u32[]{:S(2)}) collective-permute-start(bf16[4,64,512]{2,1,0:T(8,128)(2,1)S(1)} %collective-permute-done.8), channel_id=1, source_target_pairs={{1,2},{2,3},{5,6},{6,7},{9,10},{10,11},{13,14},{14,15},{17,18},{18... | collective-permute-start | bytes 786440 | tf_op jit(solution)/shard_map/ppermute | solution.py:213
  27.8 14.3 %collective-permute-start.3 = (bf16[4,64,512]{2,1,0:T(8,128)(2,1)S(1)}, bf16[4,64,512]{2,1,0:T(8,128)(2,1)S(1)}, u32[]{:S(2)}, u32[]{:S(2)}) collective-permute-start(bf16[4,64,512]{2,1,0:T(8,128)(2,1)S(1)} %collective-permute-done.2), channel_id=1, source_target_pairs={{1,0},{5,4},{9,8},{13,12},{17,16},{21,20},{25,24},{29,28}} | collective-permute-start | bytes 786440 | tf_op jit(solution)/shard_map/ppermute | solution.py:214
  29.1 13.1 %collective-permute-start.5 = (bf16[4,64,512]{2,1,0:T(8,128)(2,1)}, bf16[4,64,512]{2,1,0:T(8,128)(2,1)S(1)}, u32[]{:S(2)}, u32[]{:S(2)}) collective-permute-start(bf16[4,64,512]{2,1,0:T(8,128)(2,1)} %collective-permute-done.4), channel_id=1, source_target_pairs={{2,3},{6,7},{10,11},{14,15},{18,19},{22,23},{26,27},{30,31}} | collective-permute-start | bytes 786440 | tf_op jit(solution)/shard_map/ppermute | solution.py:213
  34.2 27.2 %collective-permute-start.11 = (bf16[4,64,512]{2,1,0:T(8,128)(2,1)S(1)}, bf16[4,64,512]{2,1,0:T(8,128)(2,1)S(1)}, u32[]{:S(2)}, u32[]{:S(2)}) collective-permute-start(bf16[4,64,512]{2,1,0:T(8,128)(2,1)S(1)} %collective-permute-done.10), channel_id=1, source_target_pairs={{1,0},{5,4},{9,8},{13,12},{17,16},{21,20},{25,24},{29,28}} | collective-permute-start | bytes 786440 | tf_op jit(solution)/shard_map/ppermute | solution.py:214
  35.5 25.9 %collective-permute-start.13 = (bf16[4,64,512]{2,1,0:T(8,128)(2,1)S(1)}, bf16[4,64,512]{2,1,0:T(8,128)(2,1)S(1)}, u32[]{:S(2)}, u32[]{:S(2)}) collective-permute-start(bf16[4,64,512]{2,1,0:T(8,128)(2,1)S(1)} %collective-permute-done.12), channel_id=1, source_target_pairs={{2,3},{6,7},{10,11},{14,15},{18,19},{22,23},{26,27},{30,31}} | collective-permute-start | bytes 786440 | tf_op jit(solution)/shard_map/ppermute | solution.py:213
  61.3 11.3 %collective-permute-start.6 = (bf16[2,64,2048]{2,1,0:T(8,128)(2,1)S(1)}, bf16[2,64,2048]{2,1,0:T(8,128)(2,1)S(1)}, u32[]{:S(2)}, u32[]{:S(2)}) collective-permute-start(bf16[2,64,2048]{2,1,0:T(8,128)(2,1)S(1)} %dynamic-slice_bitcast_fusion.1), channel_id=1, source_target_pairs={{0,4},{4,0},{8,12},{12,8},{1,5},{5,1},{9,13},{13,9},{2,6},{6,2},{1... | collective-permute-start | bytes 1572872 | tf_op jit(solution)/shard_map/ppermute | solution.py:246
  74.6 13.1 %collective-permute-start.15 = (bf16[64,2048]{1,0:T(8,128)(2,1)S(1)}, bf16[64,2048]{1,0:T(8,128)(2,1)S(1)}, u32[]{:S(2)}, u32[]{:S(2)}) collective-permute-start(bf16[64,2048]{1,0:T(8,128)(2,1)S(1)} %fusion.15), channel_id=1, source_target_pairs={{0,8},{4,12},{8,0},{12,4},{1,9},{5,13},{9,1},{13,5},{2,10},{6,14},... | collective-permute-start | bytes 786440 | tf_op jit(solution)/shard_map/ppermute | solution.py:251
  98.0 18.3 %collective-permute-start.17 = (bf16[2,64,2048]{2,1,0:T(8,128)(2,1)S(1)}, bf16[2,64,2048]{2,1,0:T(8,128)(2,1)S(1)}, u32[]{:S(2)}, u32[]{:S(2)}) collective-permute-start(bf16[2,64,2048]{2,1,0:T(8,128)(2,1)S(1)} %pad_maximum_fusion.5), channel_id=1, source_target_pairs={{0,4},{4,0},{8,12},{12,8},{1,5},{5,1},{9,13},{13,9},{2,6},{6,2},{1... | collective-permute-start | bytes 1572872 | tf_op jit(solution)/shard_map/ppermute | solution.py:246
  127.2 24.1 %collective-permute-start.29 = (bf16[4,64,512]{2,0,1:T(4,128)(2,1)S(1)}, bf16[4,64,512]{2,0,1:T(4,128)(2,1)S(1)}, u32[]{:S(2)}, u32[]{:S(2)}) collective-permute-start(bf16[4,64,512]{2,0,1:T(4,128)(2,1)S(1)} %bitcast.164), channel_id=1, source_target_pairs={{3,2},{7,6},{11,10},{15,14},{19,18},{23,22},{27,26},{31,30}} | collective-permute-start | bytes 786440 | tf_op jit(solution)/shard_map/ppermute | solution.py:239
  127.9 24.4 %collective-permute-start.26 = (bf16[4,64,512]{2,0,1:T(4,128)(2,1)S(1)}, bf16[4,64,512]{2,0,1:T(4,128)(2,1)S(1)}, u32[]{:S(2)}, u32[]{:S(2)}) collective-permute-start(bf16[4,64,512]{2,0,1:T(4,128)(2,1)S(1)} %bitcast.162), channel_id=1, source_target_pairs={{0,1},{4,5},{8,9},{12,13},{16,17},{20,21},{24,25},{28,29}} | collective-permute-start | bytes 786440 | tf_op jit(solution)/shard_map/ppermute | solution.py:239
  140.1 14.3 %collective-permute-start.23 = (bf16[4,64,512]{2,0,1:T(4,128)(2,1)S(1)}, bf16[4,64,512]{2,0,1:T(4,128)(2,1)S(1)}, u32[]{:S(2)}, u32[]{:S(2)}) collective-permute-start(bf16[4,64,512]{2,0,1:T(4,128)(2,1)S(1)} %bitcast.165), channel_id=1, source_target_pairs={{3,2},{7,6},{11,10},{15,14},{19,18},{23,22},{27,26},{31,30}} | collective-permute-start | bytes 786440 | tf_op jit(solution)/shard_map/ppermute | solution.py:239
  140.8 14.6 %collective-permute-start.20 = (bf16[4,64,512]{2,0,1:T(4,128)(2,1)S(1)}, bf16[4,64,512]{2,0,1:T(4,128)(2,1)S(1)}, u32[]{:S(2)}, u32[]{:S(2)}) collective-permute-start(bf16[4,64,512]{2,0,1:T(4,128)(2,1)S(1)} %bitcast.163), channel_id=1, source_target_pairs={{0,1},{4,5},{8,9},{12,13},{16,17},{20,21},{24,25},{28,29}} | collective-permute-start | bytes 786440 | tf_op jit(solution)/shard_map/ppermute | solution.py:239
  152.5 11.7 %collective-permute-start.27 = (bf16[4,64,512]{2,0,1:T(4,128)(2,1)S(1)}, bf16[4,64,512]{2,0,1:T(4,128)(2,1)S(1)}, u32[]{:S(2)}, u32[]{:S(2)}) collective-permute-start(bf16[4,64,512]{2,0,1:T(4,128)(2,1)S(1)} %fusion.2), channel_id=1, source_target_pairs={{0,1},{1,2},{4,5},{5,6},{8,9},{9,10},{12,13},{13,14},{16,17},{17,1... | collective-permute-start | bytes 786440 | tf_op jit(solution)/shard_map/ppermute | solution.py:239
  154.7 15.0 %collective-permute-start.24 = (bf16[4,64,512]{2,0,1:T(4,128)(2,1)S(1)}, bf16[4,64,512]{2,0,1:T(4,128)(2,1)S(1)}, u32[]{:S(2)}, u32[]{:S(2)}) collective-permute-start(bf16[4,64,512]{2,0,1:T(4,128)(2,1)S(1)} %fusion.6), channel_id=1, source_target_pairs={{3,2},{2,1},{7,6},{6,5},{11,10},{10,9},{15,14},{14,13},{19,18},{18... | collective-permute-start | bytes 786440 | tf_op jit(solution)/shard_map/ppermute | solution.py:239
  155.7 15.6 %collective-permute-start.21 = (bf16[4,64,512]{2,0,1:T(4,128)(2,1)S(1)}, bf16[4,64,512]{2,0,1:T(4,128)(2,1)S(1)}, u32[]{:S(2)}, u32[]{:S(2)}) collective-permute-start(bf16[4,64,512]{2,0,1:T(4,128)(2,1)S(1)} %fusion.8), channel_id=1, source_target_pairs={{0,1},{1,2},{4,5},{5,6},{8,9},{9,10},{12,13},{13,14},{16,17},{17,1... | collective-permute-start | bytes 786440 | tf_op jit(solution)/shard_map/ppermute | solution.py:239
  163.0 22.4 %collective-permute-start.31 = (bf16[4,64,512]{2,0,1:T(4,128)(2,1)S(1)}, bf16[4,64,512]{2,0,1:T(4,128)(2,1)S(1)}, u32[]{:S(2)}, u32[]{:S(2)}) collective-permute-start(bf16[4,64,512]{2,0,1:T(4,128)(2,1)S(1)} %fusion.1), channel_id=1, source_target_pairs={{3,2},{2,1},{1,0},{7,6},{6,5},{5,4},{11,10},{10,9},{9,8},{15,14},{... | collective-permute-start | bytes 786440 | tf_op jit(solution)/shard_map/ppermute | solution.py:239
  164.5 20.8 %collective-permute-start.28 = (bf16[4,64,512]{2,0,1:T(4,128)(2,1)S(1)}, bf16[4,64,512]{2,0,1:T(4,128)(2,1)S(1)}, u32[]{:S(2)}, u32[]{:S(2)}) collective-permute-start(bf16[4,64,512]{2,0,1:T(4,128)(2,1)S(1)} %fusion.3), channel_id=1, source_target_pairs={{0,1},{1,2},{2,3},{4,5},{5,6},{6,7},{8,9},{9,10},{10,11},{12,13},{... | collective-permute-start | bytes 786440 | tf_op jit(solution)/shard_map/ppermute | solution.py:239
  170.0 15.7 %collective-permute-start.25 = (bf16[4,64,512]{2,0,1:T(4,128)(2,1)S(1)}, bf16[4,64,512]{2,0,1:T(4,128)(2,1)S(1)}, u32[]{:S(2)}, u32[]{:S(2)}) collective-permute-start(bf16[4,64,512]{2,0,1:T(4,128)(2,1)S(1)} %fusion.7), channel_id=1, source_target_pairs={{3,2},{2,1},{1,0},{7,6},{6,5},{5,4},{11,10},{10,9},{9,8},{15,14},{... | collective-permute-start | bytes 786440 | tf_op jit(solution)/shard_map/ppermute | solution.py:239
  171.6 14.1 %collective-permute-start.22 = (bf16[4,64,512]{2,0,1:T(4,128)(2,1)S(1)}, bf16[4,64,512]{2,0,1:T(4,128)(2,1)S(1)}, u32[]{:S(2)}, u32[]{:S(2)}) collective-permute-start(bf16[4,64,512]{2,0,1:T(4,128)(2,1)S(1)} %fusion.9), channel_id=1, source_target_pairs={{0,1},{1,2},{2,3},{4,5},{5,6},{6,7},{8,9},{9,10},{10,11},{12,13},{... | collective-permute-start | bytes 786440 | tf_op jit(solution)/shard_map/ppermute | solution.py:239
  (8 other events, 66.7 us)
where the time goes:
time: 188 us; the launch traced here: 187 us
  Pallas kernels  85.3 us (45%)
  starting transfers between devices  55.3 us (29%)
  waiting for transfers between devices  30.8 us (16%)
  local copies, waits for them, and re-layouts  7.45 us (4%)
  other arithmetic  6.82 us (4%)
    pallas_call x3, Pallas kernels, outer(): pl.pallas_call(outer_kernel, grid=(latents // high,), in_specs=[pl.BlockS...  27.5 us
    ppermute x12, starting transfers between devices, reduce_tok(): got = lax.ppermute(send.astype(jnp.bfloat16), 'tok', perm)  26.9 us
    pallas_call x3, Pallas kernels, rebuild(): pl.pallas_call(rebuild_kernel, grid=(columns // wide,), in_specs=[pl.Bloc...  25.6 us
    pallas_call x2, Pallas kernels, back_compact(): pl.pallas_call(functools.partial(back_compact_kernel, rows, slots, blocks...  19.8 us
    ppermute x4, waiting for transfers between devices, row_shift(): lax.ppermute(value, 'blk', [(i, (i + 2 * k) % count) for i in range(count)])  16.7 us
    ppermute x6, waiting for transfers between devices, gather_tok(): lax.ppermute(down[-1], 'tok', [(i, i - 1) for i in range(1, count - m + 1)])  14.1 us
    ppermute x6, starting transfers between devices, gather_tok(): lax.ppermute(up[-1], 'tok', [(i, i + 1) for i in range(m - 1, count - 1)])  13.7 us
    pallas_call x1, Pallas kernels, back(): pl.pallas_call(back_kernel, grid=(latents // region_width,), in_specs=[pl...  8.77 us
  transfers between devices with their start and end apart: 32, of which 7 were waited for; matrix products, arithmetic and copies ran while one was open for 6% of the time, Pallas kernels for 40%

commit v1 on v0

v1 whole, which is shorter than its diff:
```python
import functools

import jax
import jax.numpy as jnp
from jax import lax
from jax.experimental import pallas as pl
from jax.experimental.pallas import tpu as pltpu
from jax.sharding import PartitionSpec as P

BLOCK = 64
PAIR = 2 * BLOCK
VMEM_LIMIT = 48 * 2**20


def params(dims):
    return pltpu.CompilerParams(
        dimension_semantics=("arbitrary",) * dims if dims else None, vmem_limit_bytes=VMEM_LIMIT
    )


def cost(flops, read):
    return pl.CostEstimate(flops=flops, bytes_accessed=read, transcendentals=0)


def pick_blocks(read_pair, write_pair, index, dup, sources, dests, rows):
    low = lax.broadcasted_iota(jnp.int32, (rows, PAIR), 1) < BLOCK
    for j in range(sources // 2):
        value = read_pair(j)
        turned = pltpu.roll(value, BLOCK, 1)
        dup[2 * j] = jnp.where(low, value, turned)
        dup[2 * j + 1] = jnp.where(low, turned, value)
    dup[sources] = jnp.zeros((rows, PAIR), jnp.float32)
    for j in range(dests // 2):
        write_pair(j, jnp.where(low, dup[index(2 * j)], dup[index(2 * j + 1)]))


def expand_kernel(rows, slots, blocks, inverse, order, src, out, dup):
    step = pl.program_id(0)
    regions = src.shape[1]
    tiles = src.shape[2] // rows
    first = order[step] * tiles
    width = blocks * BLOCK
    for r in range(regions):
        for x in range(tiles):
            here = pl.ds(x * rows, rows)
            base = ((first + x) * regions + r) * blocks

            def read(j):
                return src[0, r, here, pl.ds(j * PAIR, PAIR)].astype(jnp.float32)

            def write(j, value):
                out[here, pl.ds(r * width + j * PAIR, PAIR)] = value.astype(out.dtype)

            pick_blocks(read, write, lambda k: inverse[base + k], dup.at[r * tiles + x], slots, blocks, rows)


def expand(shards, inverse, order, rows, blocks):
    count, regions, own, slot_width = shards.shape
    slots = slot_width // BLOCK
    width = regions * blocks * BLOCK
    return pl.pallas_call(
        functools.partial(expand_kernel, rows, slots, blocks),
        grid_spec=pltpu.PrefetchScalarGridSpec(
            num_scalar_prefetch=2,
            grid=(count,),
            in_specs=[pl.BlockSpec((1, regions, own, slot_width), lambda k, inv, order: (k, 0, 0, 0))],
            out_specs=pl.BlockSpec((own, width), lambda k, inv, order: (order[k], 0)),
            scratch_shapes=[pltpu.VMEM((regions * own // rows, slots + 1, rows, PAIR), jnp.float32)],
        ),
        out_shape=jax.ShapeDtypeStruct((count * own, width), jnp.bfloat16),
        compiler_params=params(1),
        cost_estimate=cost(0, 6 * count * own * width),
        name="expand",
    )(inverse, order, shards)


DEPTH = 4


def stream(copies, work):
    count = len(copies)
    for i in range(min(DEPTH, count)):
        copies[i].start()
    for i in range(count):
        copies[i].wait()
        if i + DEPTH < count:
            copies[i + DEPTH].start()
        work(i)


def rebuild_kernel(pair, codes, dec, *rest):
    out, held, sems = rest[-3:]
    wide = held.shape[2]

    def work(i):
        here = pl.ds(i * wide, wide)
        total = jnp.dot(codes[...], held[i], preferred_element_type=jnp.float32)
        if len(rest) == 4:
            total = total + rest[0][:, here]
        out[:, here] = total.astype(out.dtype)

    stream(
        [
            pltpu.make_async_copy(dec.at[pair, :, pl.ds(i * wide, wide)], held.at[i], sems.at[i])
            for i in range(held.shape[0])
        ],
        work,
    )


def rebuild(codes, decoder, pair, before, dtype):
    tokens, latents = codes.shape
    columns = decoder.shape[2]
    wide = min(256, columns)
    whole = pl.BlockSpec(memory_space=pltpu.VMEM)
    ins = [codes, decoder] + ([] if before is None else [before])
    return pl.pallas_call(
        functools.partial(rebuild_kernel, pair),
        in_specs=[whole, pl.BlockSpec(memory_space=pl.ANY)] + [whole] * (len(ins) - 2),
        out_specs=whole,
        out_shape=jax.ShapeDtypeStruct((tokens, columns), dtype),
        scratch_shapes=[
            pltpu.VMEM((columns // wide, latents, wide), jnp.bfloat16),
            pltpu.SemaphoreType.DMA((columns // wide,)),
        ],
        compiler_params=params(0),
        cost_estimate=cost(2 * tokens * latents * columns, 2 * latents * columns),
        name="rebuild",
    )(*ins)


def outer_kernel(pair, codes, error, *rest):
    out, held, sems = rest[-3:]
    high = held.shape[1]
    copies = []
    for i in range(held.shape[0]):
        here = pl.ds(i * high, high)
        held[i] = lax.dot_general(
            codes[:, here], error[...], (((0,), (0,)), ((), ())), preferred_element_type=jnp.float32
        ).astype(out.dtype)
        copies.append(pltpu.make_async_copy(held.at[i], out.at[pair, here], sems.at[i]))
        copies[-1].start()
    for copy in copies:
        copy.wait()


def outer(codes, error, pair, pairs, held):
    tokens, latents = codes.shape
    columns = error.shape[1]
    high = min(512, latents)
    whole = pl.BlockSpec(memory_space=pltpu.VMEM)
    far = pl.BlockSpec(memory_space=pl.ANY)
    ins = [codes, error] + ([] if held is None else [held])
    return pl.pallas_call(
        functools.partial(outer_kernel, pair),
        in_specs=[whole, whole] + [far] * (len(ins) - 2),
        out_specs=far,
        out_shape=jax.ShapeDtypeStruct((pairs, latents, columns), jnp.bfloat16),
        input_output_aliases={} if held is None else {2: 0},
        scratch_shapes=[
            pltpu.VMEM((latents // high, high, columns), jnp.bfloat16),
            pltpu.SemaphoreType.DMA((latents // high,)),
        ],
        compiler_params=params(0),
        cost_estimate=cost(2 * tokens * latents * columns, 2 * latents * columns),
        name="outer",
    )(*ins)


def back_compact_kernel(rows, slots, blocks, regions, pairs, chosen, *rest):
    errors, (dec, out, total, dup, held, sems) = rest[: len(pairs)], rest[len(pairs):]
    high = held.shape[1]
    width = blocks * BLOCK
    parts = width // high

    def finish(r):
        for x in range(total.shape[1] // rows):
            here = pl.ds(x * rows, rows)
            base = (x * regions + r) * slots

            def read(j):
                return total[r % 2, here, pl.ds(j * PAIR, PAIR)]

            def write(j, value):
                out[r, here, pl.ds(j * PAIR, PAIR)] = value.astype(out.dtype)

            pick_blocks(read, write, lambda k: chosen[base + k], dup.at[x % 4], blocks, slots, rows)

    def work(i):
        step, which = i // len(pairs), i % len(pairs)
        r, here = step // parts, pl.ds(step % parts * high, high)
        value = lax.dot_general(
            errors[which][...], held[i], (((1,), (1,)), ((), ())), preferred_element_type=jnp.float32
        )
        if which > 0:
            value = value + total[r % 2, :, here]
        total[r % 2, :, here] = value
        if step % parts == parts - 1 and which == len(pairs) - 1:
            finish(r)

    stream(
        [
            pltpu.make_async_copy(
                dec.at[pairs[i % len(pairs)], pl.ds(i // len(pairs) * high, high)], held.at[i], sems.at[i]
            )
            for i in range(held.shape[0])
        ],
        work,
    )


def back_compact(errors, decoder, pairs, chosen, rows, slots, regions):
    tokens, columns = errors[0].shape
    latents = decoder.shape[1]
    width = latents // regions
    blocks = width // BLOCK
    high = min(512, width)
    steps = latents // high * len(pairs)
    whole = pl.BlockSpec(memory_space=pltpu.VMEM)
    return pl.pallas_call(
        functools.partial(back_compact_kernel, rows, slots, blocks, regions, pairs),
        in_specs=[pl.BlockSpec(memory_space=pltpu.SMEM)]
        + [whole] * len(pairs)
        + [pl.BlockSpec(memory_space=pl.ANY)],
        out_specs=whole,
        out_shape=jax.ShapeDtypeStruct((regions, tokens, slots * BLOCK), jnp.bfloat16),
        scratch_shapes=[
            pltpu.VMEM((2, tokens, width), jnp.float32),
            pltpu.VMEM((4, blocks + 1, rows, PAIR), jnp.float32),
            pltpu.VMEM((steps, high, columns), jnp.bfloat16),
            pltpu.SemaphoreType.DMA((steps,)),
        ],
        compiler_params=params(0),
        cost_estimate=cost(
            2 * len(pairs) * tokens * latents * columns, 2 * len(pairs) * latents * columns
        ),
        name="back_compact",
    )(chosen, *errors, decoder)


def tok_shift(value, k):
    count = lax.axis_size("tok")
    return lax.ppermute(value, "tok", [(i, (i + k) % count) for i in range(count)])


def gather_tok(own):
    count = lax.axis_size("tok")
    return jnp.stack([own] + [tok_shift(own, k) for k in range(1, count)])


def reduce_tok(parts):
    count = lax.axis_size("tok")
    me = lax.axis_index("tok")

    def chunk(k):
        return lax.dynamic_index_in_dim(parts, (me + k) % count, 1, keepdims=False)

    got = [tok_shift(chunk(k), k) for k in range(1, count)]
    total = chunk(0).astype(jnp.float32)
    for value in got:
        total = total + value.astype(jnp.float32)
    return total.astype(jnp.bfloat16)


def core_swap(value):
    count = lax.axis_size("blk")
    return lax.ppermute(value, "blk", [(i, i ^ 1) for i in range(count)])


def row_shift(value, k):
    count = lax.axis_size("blk")
    return lax.ppermute(value, "blk", [(i, (i + 2 * k) % count) for i in range(count)])


def reduce_blk(part):
    count = lax.axis_size("blk")
    me = lax.axis_index("blk")
    core, row, chips = me % 2, me // 2, count // 2
    tokens, columns = part.shape
    split = part.reshape(chips, 2, tokens // count, columns)
    send = lax.dynamic_index_in_dim(split, 1 - core, 1, keepdims=False)
    kept = lax.dynamic_index_in_dim(split, core, 1, keepdims=False)
    both = kept.astype(jnp.float32) + core_swap(send).astype(jnp.float32)

    def shard(r):
        return lax.dynamic_index_in_dim(both, r, 0, keepdims=False)

    total = shard(row)
    for k in range(1, chips):
        sent = shard((row + k) % chips).astype(jnp.bfloat16)
        total = total + row_shift(sent, k).astype(jnp.float32)
    return total


def gather_blk(own):
    count = lax.axis_size("blk")
    me = lax.axis_index("blk")
    core, row, chips = me % 2, me // 2, count // 2
    held = [own] + [row_shift(own, k) for k in range(1, chips)]
    mine = []
    for r in range(chips):
        value = held[0]
        for k in range(1, chips):
            value = jnp.where((row - k + chips) % chips == r, held[k], value)
        mine.append(value)
    mine = jnp.stack(mine)
    other = core_swap(mine)
    even = jnp.where(core == 0, mine, other)
    odd = jnp.where(core == 0, other, mine)
    return jnp.stack([even, odd], 1).reshape(count * own.shape[0], own.shape[1])


def per_device(latent_codes, block_lists, block_counts, decoder, targets):
    own_rows, layers, regions, slot_width = latent_codes.shape
    slots = block_lists.shape[3]
    latents = decoder.shape[1]
    region_width = latents // regions
    blocks = region_width // BLOCK
    count = lax.axis_size("tok")
    tokens = count * own_rows
    rows = tokens // block_lists.shape[0]
    me = lax.axis_index("tok")

    own = latent_codes.transpose(1, 2, 0, 3)
    gathered0 = gather_tok(own[0])
    gathered0, own1 = lax.optimization_barrier((gathered0, own[1]))
    gathered = [gathered0, gather_tok(own1)]

    active = lax.broadcasted_iota(jnp.int32, block_lists.shape, 3) < block_counts[..., None]
    chosen = jnp.where(active, block_lists, blocks)
    slot = lax.broadcasted_iota(jnp.int32, block_lists.shape + (blocks,), 3)
    block = lax.broadcasted_iota(jnp.int32, block_lists.shape + (blocks,), 4)
    inverse = jnp.min(jnp.where(chosen[..., None] == block, slot, slots), axis=3)
    order = (me - jnp.arange(count, dtype=jnp.int32) + count) % count

    codes = [
        expand(gathered[s], inverse[:, s].reshape(-1), order, rows, blocks) for s in range(layers)
    ]

    part0 = rebuild(codes[0], decoder, 0, None, jnp.bfloat16)
    part0, codes0 = lax.optimization_barrier((part0, codes[0]))
    partial = rebuild(codes0, decoder, 1, None, jnp.float32)
    part1 = rebuild(codes[1], decoder, 2, partial, jnp.bfloat16)

    def error_of(part, t):
        return (reduce_blk(part) - targets[:, t].astype(jnp.float32)).astype(jnp.bfloat16)

    own_error = [error_of(part0, 0), error_of(part1, 1)]
    recon_error = jnp.stack(own_error, 1)
    error = [gather_blk(e) for e in own_error]

    grads = outer(codes[0], error[0], 0, decoder.shape[0], None)

    def codes_grad(errors, pairs, s):
        packed = back_compact(
            errors, decoder, pairs, chosen[:, s].reshape(-1), rows, slots, regions
        )
        return reduce_tok(packed.reshape(regions, count, own_rows, slot_width))

    grad1 = codes_grad([error[1]], [2], 1)
    grad0 = codes_grad(error, [0, 1], 0)
    grads = outer(codes[0], error[1], 1, decoder.shape[0], grads)
    grads = outer(codes[1], error[1], 2, decoder.shape[0], grads)
    code_grad = jnp.stack([grad0, grad1], 0).transpose(2, 0, 1, 3)
    return (recon_error, grads, code_grad)


def solution(mesh):
    placed = (
        P(("groups", "tok"), None, "blk", None),
        P("groups", None, "blk", None),
        P("groups", None, "blk"),
        P(None, "blk", "tok"),
        P(("groups", "blk"), None, "tok"),
    )
    return jax.shard_map(
        per_device,
        mesh=mesh,
        in_specs=placed,
        out_specs=(
            P(("groups", "blk"), None, "tok"),
            P("groups", "blk", "tok"),
            P(("groups", "tok"), None, "blk", None),
        ),
        check_vma=False,
    )
```

time: 188 us -> 183 us (0.973)
  the two profiles are of different devices: /device:TPU:0 before, /device:TPU:26 now
where the time goes in v1:
time: 183 us; the launch traced here: 180 us
  Pallas kernels  82.4 us (45%)
  waiting for transfers between devices  57.1 us (31%)
  starting transfers between devices  27.2 us (15%)
  local copies, waits for them, and re-layouts  7.66 us (4%)
  other arithmetic  4.72 us (3%)
    ppermute x12, waiting for transfers between devices, tok_shift(): lax.ppermute(value, 'tok', [(i, (i + k) % count) for i in range(count)])  40.3 us
    pallas_call x3, Pallas kernels, rebuild(): pl.pallas_call(functools.partial(rebuild_kernel, pair), in_specs=[whole,...  34.5 us
    pallas_call x2, Pallas kernels, back_compact(): pl.pallas_call(functools.partial(back_compact_kernel, rows, slots, blocks...  24.2 us
    ppermute x12, starting transfers between devices, tok_shift(): lax.ppermute(value, 'tok', [(i, (i + k) % count) for i in range(count)])  20.3 us
    pallas_call x3, Pallas kernels, outer(): pl.pallas_call(functools.partial(outer_kernel, pair), in_specs=[whole, wh...  20 us
    ppermute x4, waiting for transfers between devices, row_shift(): lax.ppermute(value, 'blk', [(i, (i + 2 * k) % count) for i in range(count)])  16.8 us
    ppermute x4, starting transfers between devices, row_shift(): lax.ppermute(value, 'blk', [(i, (i + 2 * k) % count) for i in range(count)])  6.09 us
    pallas_call x2, Pallas kernels, expand(): pl.pallas_call(functools.partial(expand_kernel, rows, slots, blocks), gri...  3.74 us
  transfers between devices with their start and end apart: 20, of which 8 were waited for; matrix products, arithmetic and copies ran while one was open for 4% of the time, Pallas kernels for 32%

profile of v1, /device:TPU:26, one launch (start us, length us, event | category | flops | bytes accessed | tf_op | source)
XLA Modules:
  0.0 180.4 jit_solution(3589059185442919138)
XLA Ops:
  2.7 3.0 %collective-permute-start = (bf16[4,64,512]{2,1,0:T(8,128)(2,1)S(1)}, bf16[4,64,512]{2,1,0:T(8,128)(2,1)S(1)}, u32[]{:S(2)}, u32[]{:S(2)}) collective-permute-start(bf16[4,64,512]{2,1,0:T(8,128)(2,1)S(1)} %get-tuple-element.36), channel_id=1, source_target_pairs={{0,1},{1,2},{2,3},{3,0},{4,5},{5,6},{6,7},{7,4},{8,9},{9,10},{10,1... | collective-permute-start | bytes 786440 | tf_op jit(solution)/shard_map/ppermute | solution.py:243
  7.7 2.1 %fusion.14 = (bf16[64,1,2048]{2,1,0:T(2,128)(2,1)S(1)}, bf16[64,1,2048]{2,1,0:T(2,128)(2,1)S(1)}) fusion(bf16[64,2,2048]{2,1,0:T(2,128)(2,1)} %param.9), kind=kLoop, calls=%fused_computation.69 | loop fusion | bytes 1048576 | tf_op jit(solution)/shard_map/slice | solution.py:346
  10.2 2.9 %collective-permute-done.2 = bf16[4,64,512]{2,1,0:T(8,128)(2,1)S(1)} collective-permute-done((bf16[4,64,512]{2,1,0:T(8,128)(2,1)S(1)}, bf16[4,64,512]{2,1,0:T(8,128)(2,1)S(1)}, u32[]{:S(2)}, u32[]{:S(2)}) %collective-permute-start.2) | collective-permute-done | bytes 262176 | tf_op jit(solution)/shard_map/ppermute | solution.py:243
  13.0 10.2 %collective-permute-done.1 = bf16[4,64,512]{2,1,0:T(8,128)(2,1)S(1)} collective-permute-done((bf16[4,64,512]{2,1,0:T(8,128)(2,1)S(1)}, bf16[4,64,512]{2,1,0:T(8,128)(2,1)S(1)}, u32[]{:S(2)}, u32[]{:S(2)}) %collective-permute-start.1) | collective-permute-done | bytes 262176 | tf_op jit(solution)/shard_map/ppermute | solution.py:243
  23.4 5.4 %collective-permute-start.7 = (bf16[4,64,512]{2,1,0:T(8,128)(2,1)S(1)}, bf16[4,64,512]{2,1,0:T(8,128)(2,1)S(1)}, u32[]{:S(2)}, u32[]{:S(2)}) collective-permute-start(bf16[4,64,512]{2,1,0:T(8,128)(2,1)S(1)} %get-tuple-element.9), channel_id=1, source_target_pairs={{0,3},{1,0},{2,1},{3,2},{4,7},{5,4},{6,5},{7,6},{8,11},{9,8},{10,9... | collective-permute-start | bytes 786440 | tf_op jit(solution)/shard_map/ppermute | solution.py:243
  28.8 2.8 %collective-permute-start.5 = (bf16[4,64,512]{2,1,0:T(8,128)(2,1)S(1)}, bf16[4,64,512]{2,1,0:T(8,128)(2,1)S(1)}, u32[]{:S(2)}, u32[]{:S(2)}) collective-permute-start(bf16[4,64,512]{2,1,0:T(8,128)(2,1)S(1)} %get-tuple-element.9), channel_id=1, source_target_pairs={{0,1},{1,2},{2,3},{3,0},{4,5},{5,6},{6,7},{7,4},{8,9},{9,10},{10,1... | collective-permute-start | bytes 786440 | tf_op jit(solution)/shard_map/ppermute | solution.py:243
  31.7 1.8 expand.2.codes
  33.5 11.5 %rebuild.3 = bf16[256,2048]{1,0:T(8,128)(2,1)S(1)} custom-call(bf16[256,4096]{1,0:T(8,128)(2,1)S(1)} %expand.2.codes, bf16[3,4096,2048]{2,1,0:T(8,128)(2,1)} %rest_1_.1), custom_call_target="tpu_custom_call" | custom-call | flops 4294967296 | bytes 16777216 | tf_op jit(solution)/shard_map/rebuild/pallas_call | solution.py:117
  45.1 11.5 %rebuild.4.rest_0_ = f32[256,2048]{1,0:T(8,128)S(1)} custom-call(bf16[256,4096]{1,0:T(8,128)(2,1)S(1)} %expand.2.codes, bf16[3,4096,2048]{2,1,0:T(8,128)(2,1)} %rest_1_.1), custom_call_target="tpu_custom_call" | custom-call | flops 4294967296 | bytes 16777216 | tf_op jit(solution)/shard_map/rebuild/pallas_call | solution.py:117
  56.8 2.0 %expand.3.codes = bf16[256,4096]{1,0:T(8,128)(2,1)S(1)} custom-call(s32[512]{0:T(512)S(1)} %reshape_squeeze.13.inverse, s32[4]{0:T(128)S(1)} %and_select_fusion.order, bf16[4,4,64,512]{3,2,1,0:T(8,128)(2,1)S(1)} %pad_maximum_fusion.1.src), custom_call_target="tpu_custom_call" | custom-call | bytes 6291456 | tf_op jit(solution)/shard_map/expand/pallas_call | solution.py:61
  58.7 11.5 %rebuild.5 = bf16[256,2048]{1,0:T(8,128)(2,1)S(1)} custom-call(bf16[256,4096]{1,0:T(8,128)(2,1)S(1)} %expand.3.codes, bf16[3,4096,2048]{2,1,0:T(8,128)(2,1)} %rest_1_.1, f32[256,2048]{1,0:T(8,128)S(1)} %rebuild.4.rest_0_), custom_call_target="tpu_custom_call" | custom-call | flops 4294967296 | bytes 16777216 | tf_op jit(solution)/shard_map/rebuild/pallas_call | solution.py:117
  74.2 6.1 %collective-permute-done.4 = bf16[64,2048]{1,0:T(8,128)(2,1)S(1)} collective-permute-done((bf16[64,2048]{1,0:T(8,128)(2,1)S(1)}, bf16[64,2048]{1,0:T(8,128)(2,1)S(1)}, u32[]{:S(2)}, u32[]{:S(2)}) %collective-permute-start.4) | collective-permute-done | bytes 262176 | tf_op jit(solution)/shard_map/ppermute | solution.py:272
  82.1 3.8 %collective-permute-done.9 = bf16[64,2048]{1,0:T(8,128)(2,1)S(1)} collective-permute-done((bf16[64,2048]{1,0:T(8,128)(2,1)S(1)}, bf16[64,2048]{1,0:T(8,128)(2,1)S(1)}, u32[]{:S(2)}, u32[]{:S(2)}) %collective-permute-start.9) | collective-permute-done | bytes 262176 | tf_op jit(solution)/shard_map/ppermute | solution.py:272
  87.7 3.8 %collective-permute-done.12 = bf16[64,2048]{1,0:T(8,128)(2,1)S(1)} collective-permute-done((bf16[64,2048]{1,0:T(8,128)(2,1)S(1)}, bf16[64,2048]{1,0:T(8,128)(2,1)S(1)}, u32[]{:S(2)}, u32[]{:S(2)}) %collective-permute-start.12) | collective-permute-done | bytes 262176 | tf_op jit(solution)/shard_map/ppermute | solution.py:272
  93.1 3.1 %collective-permute-done.10 = bf16[64,2048]{1,0:T(8,128)(2,1)S(1)} collective-permute-done((bf16[64,2048]{1,0:T(8,128)(2,1)S(1)}, bf16[64,2048]{1,0:T(8,128)(2,1)S(1)}, u32[]{:S(2)}, u32[]{:S(2)}) %collective-permute-start.10) | collective-permute-done | bytes 262176 | tf_op jit(solution)/shard_map/ppermute | solution.py:272
  96.7 6.7 %outer.3.rest_0_ = bf16[3,4096,2048]{2,1,0:T(8,128)(2,1)} custom-call(bf16[256,4096]{1,0:T(8,128)(2,1)S(1)} %expand.2.codes, bf16[256,2048]{1,0:T(8,128)(2,1)S(1)} %bitcast.112), custom_call_target="tpu_custom_call" | custom-call | flops 4294967296 | bytes 16777216 | tf_op jit(solution)/shard_map/outer/pallas_call | solution.py:154
  103.9 9.3 %back_compact.3 = bf16[4,256,512]{2,1,0:T(8,128)(2,1)S(1)} custom-call(s32[256]{0:T(256)S(1)} %reshape_squeeze.15.chosen, bf16[256,2048]{1,0:T(8,128)(2,1)S(1)} %bitcast.108, bf16[3,4096,2048]{2,1,0:T(8,128)(2,1)} %rest_1_.1), custom_call_target="tpu_custom_call" | custom-call | flops 4294967296 | bytes 16777216 | tf_op jit(solution)/shard_map/back_compact/pallas_call | solution.py:220
  113.2 14.9 %back_compact.2 = bf16[4,256,512]{2,1,0:T(8,128)(2,1)S(1)} custom-call(s32[256]{0:T(256)S(1)} %reshape_squeeze.14.chosen, bf16[256,2048]{1,0:T(8,128)(2,1)S(1)} %bitcast.113, bf16[256,2048]{1,0:T(8,128)(2,1)S(1)} %bitcast.109, bf16[3,4096,2048]{2,1,0:T(8,128)(2,1)} %rest_1_.1), custom_call_target="tpu_custom_call" | custom-call | flops 8589934592 | bytes 33554432 | tf_op jit(solution)/shard_map/back_compact/pallas_call | solution.py:220
  129.6 2.5 %collective-permute-start.15 = (bf16[4,64,512]{2,0,1:T(4,128)(2,1)S(1)}, bf16[4,64,512]{2,0,1:T(4,128)(2,1)S(1)}, u32[]{:S(2)}, u32[]{:S(2)}) collective-permute-start(bf16[4,64,512]{2,0,1:T(4,128)(2,1)S(1)} %bitcast.128), channel_id=1, source_target_pairs={{0,2},{1,3},{2,0},{3,1},{4,6},{5,7},{6,4},{7,5},{8,10},{9,11},{10,... | collective-permute-start | bytes 786440 | tf_op jit(solution)/shard_map/ppermute | solution.py:243
  135.6 6.7 %outer.4.rest_0_ = bf16[3,4096,2048]{2,1,0:T(8,128)(2,1)} custom-call(bf16[256,4096]{1,0:T(8,128)(2,1)S(1)} %expand.2.codes, bf16[256,2048]{1,0:T(8,128)(2,1)S(1)} %bitcast.110, bf16[3,4096,2048]{2,1,0:T(8,128)(2,1)} %outer.3.rest_0_), custom_call_target="tpu_custom_call", output_to_operand_aliasing={{}: (2, {})} | custom-call | flops 4294967296 | bytes 16777216 | tf_op jit(solution)/shard_map/outer/pallas_call | solution.py:154
  142.3 2.1 %collective-permute-start.19 = (bf16[4,64,512]{2,0,1:T(4,128)(2,1)S(1)}, bf16[4,64,512]{2,0,1:T(4,128)(2,1)S(1)}, u32[]{:S(2)}, u32[]{:S(2)}) collective-permute-start(bf16[4,64,512]{2,0,1:T(4,128)(2,1)S(1)} %bitcast.124), channel_id=1, source_target_pairs={{0,3},{1,0},{2,1},{3,2},{4,7},{5,4},{6,5},{7,6},{8,11},{9,8},{10,9... | collective-permute-start | bytes 786440 | tf_op jit(solution)/shard_map/ppermute | solution.py:243
  144.4 6.7 %outer.5 = bf16[3,4096,2048]{2,1,0:T(8,128)(2,1)} custom-call(bf16[256,4096]{1,0:T(8,128)(2,1)S(1)} %expand.3.codes, bf16[256,2048]{1,0:T(8,128)(2,1)S(1)} %bitcast.111, bf16[3,4096,2048]{2,1,0:T(8,128)(2,1)} %outer.4.rest_0_), custom_call_target="tpu_custom_call", output_to_operand_aliasing={{}: (2, {})} | custom-call | flops 4294967296 | bytes 16777216 | tf_op jit(solution)/shard_map/outer/pallas_call | solution.py:154
  151.5 4.6 %collective-permute-done.17 = bf16[4,64,512]{2,0,1:T(4,128)(2,1)S(1)} collective-permute-done((bf16[4,64,512]{2,0,1:T(4,128)(2,1)S(1)}, bf16[4,64,512]{2,0,1:T(4,128)(2,1)S(1)}, u32[]{:S(2)}, u32[]{:S(2)}) %collective-permute-start.17) | collective-permute-done | bytes 262176 | tf_op jit(solution)/shard_map/ppermute | solution.py:243
  156.1 22.6 %collective-permute-done.18 = bf16[4,64,512]{2,0,1:T(4,128)(2,1)S(1)} collective-permute-done((bf16[4,64,512]{2,0,1:T(4,128)(2,1)S(1)}, bf16[4,64,512]{2,0,1:T(4,128)(2,1)S(1)}, u32[]{:S(2)}, u32[]{:S(2)}) %collective-permute-start.18) | collective-permute-done | bytes 262176 | tf_op jit(solution)/shard_map/ppermute | solution.py:243
  (71 shorter events, 21.6 us)
Async XLA Ops:
  1.9 11.1 %collective-permute-start.2 = (bf16[4,64,512]{2,1,0:T(8,128)(2,1)S(1)}, bf16[4,64,512]{2,1,0:T(8,128)(2,1)S(1)}, u32[]{:S(2)}, u32[]{:S(2)}) collective-permute-start(bf16[4,64,512]{2,1,0:T(8,128)(2,1)S(1)} %get-tuple-element.36), channel_id=1, source_target_pairs={{0,3},{1,0},{2,1},{3,2},{4,7},{5,4},{6,5},{7,6},{8,11},{9,8},{10,9... | collective-permute-start | bytes 786440 | tf_op jit(solution)/shard_map/ppermute | solution.py:243
  2.4 20.8 %collective-permute-start.1 = (bf16[4,64,512]{2,1,0:T(8,128)(2,1)S(1)}, bf16[4,64,512]{2,1,0:T(8,128)(2,1)S(1)}, u32[]{:S(2)}, u32[]{:S(2)}) collective-permute-start(bf16[4,64,512]{2,1,0:T(8,128)(2,1)S(1)} %get-tuple-element.36), channel_id=1, source_target_pairs={{0,2},{1,3},{2,0},{3,1},{4,6},{5,7},{6,4},{7,5},{8,10},{9,11},{10,... | collective-permute-start | bytes 786440 | tf_op jit(solution)/shard_map/ppermute | solution.py:243
  2.7 20.5 %collective-permute-start = (bf16[4,64,512]{2,1,0:T(8,128)(2,1)S(1)}, bf16[4,64,512]{2,1,0:T(8,128)(2,1)S(1)}, u32[]{:S(2)}, u32[]{:S(2)}) collective-permute-start(bf16[4,64,512]{2,1,0:T(8,128)(2,1)S(1)} %get-tuple-element.36), channel_id=1, source_target_pairs={{0,1},{1,2},{2,3},{3,0},{4,5},{5,6},{6,7},{7,4},{8,9},{9,10},{10,1... | collective-permute-start | bytes 786440 | tf_op jit(solution)/shard_map/ppermute | solution.py:243
  23.4 33.2 %collective-permute-start.7 = (bf16[4,64,512]{2,1,0:T(8,128)(2,1)S(1)}, bf16[4,64,512]{2,1,0:T(8,128)(2,1)S(1)}, u32[]{:S(2)}, u32[]{:S(2)}) collective-permute-start(bf16[4,64,512]{2,1,0:T(8,128)(2,1)S(1)} %get-tuple-element.9), channel_id=1, source_target_pairs={{0,3},{1,0},{2,1},{3,2},{4,7},{5,4},{6,5},{7,6},{8,11},{9,8},{10,9... | collective-permute-start | bytes 786440 | tf_op jit(solution)/shard_map/ppermute | solution.py:243
  28.7 27.9 %collective-permute-start.6 = (bf16[4,64,512]{2,1,0:T(8,128)(2,1)S(1)}, bf16[4,64,512]{2,1,0:T(8,128)(2,1)S(1)}, u32[]{:S(2)}, u32[]{:S(2)}) collective-permute-start(bf16[4,64,512]{2,1,0:T(8,128)(2,1)S(1)} %get-tuple-element.9), channel_id=1, source_target_pairs={{0,2},{1,3},{2,0},{3,1},{4,6},{5,7},{6,4},{7,5},{8,10},{9,11},{10,... | collective-permute-start | bytes 786440 | tf_op jit(solution)/shard_map/ppermute | solution.py:243
  28.8 27.8 %collective-permute-start.5 = (bf16[4,64,512]{2,1,0:T(8,128)(2,1)S(1)}, bf16[4,64,512]{2,1,0:T(8,128)(2,1)S(1)}, u32[]{:S(2)}, u32[]{:S(2)}) collective-permute-start(bf16[4,64,512]{2,1,0:T(8,128)(2,1)S(1)} %get-tuple-element.9), channel_id=1, source_target_pairs={{0,1},{1,2},{2,3},{3,0},{4,5},{5,6},{6,7},{7,4},{8,9},{9,10},{10,1... | collective-permute-start | bytes 786440 | tf_op jit(solution)/shard_map/ppermute | solution.py:243
  45.0 25.9 %collective-permute-start.3 = (bf16[2,64,2048]{2,1,0:T(8,128)(2,1)S(1)}, bf16[2,64,2048]{2,1,0:T(8,128)(2,1)S(1)}, u32[]{:S(2)}, u32[]{:S(2)}) collective-permute-start(bf16[2,64,2048]{2,1,0:T(8,128)(2,1)S(1)} %dynamic-slice_bitcast_fusion.1), channel_id=1, source_target_pairs={{0,4},{4,0},{8,12},{12,8},{1,5},{5,1},{9,13},{13,9},{2,6},{6,2},{1... | collective-permute-start | bytes 1572872 | tf_op jit(solution)/shard_map/ppermute | solution.py:267
  70.3 2.3 %collective-permute-start.8 = (bf16[2,64,2048]{2,1,0:T(8,128)(2,1)S(1)}, bf16[2,64,2048]{2,1,0:T(8,128)(2,1)S(1)}, u32[]{:S(2)}, u32[]{:S(2)}) collective-permute-start(bf16[2,64,2048]{2,1,0:T(8,128)(2,1)S(1)} %dynamic-slice_bitcast_fusion), channel_id=1, source_target_pairs={{0,4},{4,0},{8,12},{12,8},{1,5},{5,1},{9,13},{13,9},{2,6},{6,2},{1... | collective-permute-start | bytes 1572872 | tf_op jit(solution)/shard_map/ppermute | solution.py:267
  71.1 9.2 %collective-permute-start.4 = (bf16[64,2048]{1,0:T(8,128)(2,1)S(1)}, bf16[64,2048]{1,0:T(8,128)(2,1)S(1)}, u32[]{:S(2)}, u32[]{:S(2)}) collective-permute-start(bf16[64,2048]{1,0:T(8,128)(2,1)S(1)} %fusion.8), channel_id=1, source_target_pairs={{0,8},{4,12},{8,0},{12,4},{1,9},{5,13},{9,1},{13,5},{2,10},{6,14},... | collective-permute-start | bytes 786440 | tf_op jit(solution)/shard_map/ppermute | solution.py:272
  72.8 13.1 %collective-permute-start.9 = (bf16[64,2048]{1,0:T(8,128)(2,1)S(1)}, bf16[64,2048]{1,0:T(8,128)(2,1)S(1)}, u32[]{:S(2)}, u32[]{:S(2)}) collective-permute-start(bf16[64,2048]{1,0:T(8,128)(2,1)S(1)} %fusion.9), channel_id=1, source_target_pairs={{0,8},{4,12},{8,0},{12,4},{1,9},{5,13},{9,1},{13,5},{2,10},{6,14},... | collective-permute-start | bytes 786440 | tf_op jit(solution)/shard_map/ppermute | solution.py:272
  80.5 11.0 %collective-permute-start.12 = (bf16[64,2048]{1,0:T(8,128)(2,1)S(1)}, bf16[64,2048]{1,0:T(8,128)(2,1)S(1)}, u32[]{:S(2)}, u32[]{:S(2)}) collective-permute-start(bf16[64,2048]{1,0:T(8,128)(2,1)S(1)} %fusion.7), channel_id=1, source_target_pairs={{0,8},{4,12},{8,0},{12,4},{1,9},{5,13},{9,1},{13,5},{2,10},{6,14},... | collective-permute-start | bytes 786440 | tf_op jit(solution)/shard_map/ppermute | solution.py:272
  86.1 10.1 %collective-permute-start.10 = (bf16[64,2048]{1,0:T(8,128)(2,1)S(1)}, bf16[64,2048]{1,0:T(8,128)(2,1)S(1)}, u32[]{:S(2)}, u32[]{:S(2)}) collective-permute-start(bf16[64,2048]{1,0:T(8,128)(2,1)S(1)} %fusion.6), channel_id=1, source_target_pairs={{0,8},{4,12},{8,0},{12,4},{1,9},{5,13},{9,1},{13,5},{2,10},{6,14},... | collective-permute-start | bytes 786440 | tf_op jit(solution)/shard_map/ppermute | solution.py:272
  91.6 4.8 %collective-permute-start.13 = (bf16[2,64,2048]{2,1,0:T(8,128)(2,1)S(1)}, bf16[2,64,2048]{2,1,0:T(8,128)(2,1)S(1)}, u32[]{:S(2)}, u32[]{:S(2)}) collective-permute-start(bf16[2,64,2048]{2,1,0:T(8,128)(2,1)S(1)} %pad_maximum_fusion.6), channel_id=1, source_target_pairs={{0,4},{4,0},{8,12},{12,8},{1,5},{5,1},{9,13},{13,9},{2,6},{6,2},{1... | collective-permute-start | bytes 1572872 | tf_op jit(solution)/shard_map/ppermute | solution.py:267
  96.3 7.1 %collective-permute-start.11 = (bf16[2,64,2048]{2,1,0:T(8,128)(2,1)S(1)}, bf16[2,64,2048]{2,1,0:T(8,128)(2,1)S(1)}, u32[]{:S(2)}, u32[]{:S(2)}) collective-permute-start(bf16[2,64,2048]{2,1,0:T(8,128)(2,1)S(1)} %pad_maximum_fusion.5), channel_id=1, source_target_pairs={{0,4},{4,0},{8,12},{12,8},{1,5},{5,1},{9,13},{13,9},{2,6},{6,2},{1... | collective-permute-start | bytes 1572872 | tf_op jit(solution)/shard_map/ppermute | solution.py:267
  129.5 12.7 %collective-permute-start.16 = (bf16[4,64,512]{2,0,1:T(4,128)(2,1)S(1)}, bf16[4,64,512]{2,0,1:T(4,128)(2,1)S(1)}, u32[]{:S(2)}, u32[]{:S(2)}) collective-permute-start(bf16[4,64,512]{2,0,1:T(4,128)(2,1)S(1)} %bitcast.129), channel_id=1, source_target_pairs={{0,3},{1,0},{2,1},{3,2},{4,7},{5,4},{6,5},{7,6},{8,11},{9,8},{10,9... | collective-permute-start | bytes 786440 | tf_op jit(solution)/shard_map/ppermute | solution.py:243
  129.6 21.5 %collective-permute-start.15 = (bf16[4,64,512]{2,0,1:T(4,128)(2,1)S(1)}, bf16[4,64,512]{2,0,1:T(4,128)(2,1)S(1)}, u32[]{:S(2)}, u32[]{:S(2)}) collective-permute-start(bf16[4,64,512]{2,0,1:T(4,128)(2,1)S(1)} %bitcast.128), channel_id=1, source_target_pairs={{0,2},{1,3},{2,0},{3,1},{4,6},{5,7},{6,4},{7,5},{8,10},{9,11},{10,... | collective-permute-start | bytes 786440 | tf_op jit(solution)/shard_map/ppermute | solution.py:243
  132.1 19.0 %collective-permute-start.14 = (bf16[4,64,512]{2,0,1:T(4,128)(2,1)S(1)}, bf16[4,64,512]{2,0,1:T(4,128)(2,1)S(1)}, u32[]{:S(2)}, u32[]{:S(2)}) collective-permute-start(bf16[4,64,512]{2,0,1:T(4,128)(2,1)S(1)} %bitcast.127), channel_id=1, source_target_pairs={{0,1},{1,2},{2,3},{3,0},{4,5},{5,6},{6,7},{7,4},{8,9},{9,10},{10,1... | collective-permute-start | bytes 786440 | tf_op jit(solution)/shard_map/ppermute | solution.py:243
  133.4 22.7 %collective-permute-start.17 = (bf16[4,64,512]{2,0,1:T(4,128)(2,1)S(1)}, bf16[4,64,512]{2,0,1:T(4,128)(2,1)S(1)}, u32[]{:S(2)}, u32[]{:S(2)}) collective-permute-start(bf16[4,64,512]{2,0,1:T(4,128)(2,1)S(1)} %bitcast.126), channel_id=1, source_target_pairs={{0,1},{1,2},{2,3},{3,0},{4,5},{5,6},{6,7},{7,4},{8,9},{9,10},{10,1... | collective-permute-start | bytes 786440 | tf_op jit(solution)/shard_map/ppermute | solution.py:243
  134.0 44.6 %collective-permute-start.18 = (bf16[4,64,512]{2,0,1:T(4,128)(2,1)S(1)}, bf16[4,64,512]{2,0,1:T(4,128)(2,1)S(1)}, u32[]{:S(2)}, u32[]{:S(2)}) collective-permute-start(bf16[4,64,512]{2,0,1:T(4,128)(2,1)S(1)} %bitcast.125), channel_id=1, source_target_pairs={{0,2},{1,3},{2,0},{3,1},{4,6},{5,7},{6,4},{7,5},{8,10},{9,11},{10,... | collective-permute-start | bytes 786440 | tf_op jit(solution)/shard_map/ppermute | solution.py:243
  142.3 36.4 %collective-permute-start.19 = (bf16[4,64,512]{2,0,1:T(4,128)(2,1)S(1)}, bf16[4,64,512]{2,0,1:T(4,128)(2,1)S(1)}, u32[]{:S(2)}, u32[]{:S(2)}) collective-permute-start(bf16[4,64,512]{2,0,1:T(4,128)(2,1)S(1)} %bitcast.124), channel_id=1, source_target_pairs={{0,3},{1,0},{2,1},{3,2},{4,7},{5,4},{6,5},{7,6},{8,11},{9,8},{10,9... | collective-permute-start | bytes 786440 | tf_op jit(solution)/shard_map/ppermute | solution.py:243
